TPU v7x, 512 devices: a whole 4x8x8 slice. The times are simulated.
512 devices in a mesh: vox: 128 (over y, z, core), ch: 4 (over x).
Axes of the slice: x: 4, y: 8, z: 8, core: 2. Of those that a mesh axis runs over, the one named last changes fastest.
Arguments:
- fine_feat: bfloat16 [1024, 256, 256], P('vox', 'ch'), may hold values from -120 to 120
- conv_weight: bfloat16 [8, 256, 256], P(None, 'ch'), may hold values from -0.375 to 0.375
- norm_gain: float32 [256], P('ch'), may hold values from 0.5 to 2
- norm_bias: float32 [256], P('ch'), may hold values from -3 to 3
- send_row: int32 [983040], P('vox'), may hold values from -1 to 2047, as said below
- recv_row: int32 [983040], P('vox'), may hold values from -1 to 1023, as said below
Outputs:
- coarse_out: bfloat16 [256, 131072], P('ch', 'vox')
Inputs may be any that keep to these rules, and one draw needn't show every extreme that they name: `send_row`: within each peer group of a device the live entries come first; at most 1536 live entries, the group e = 2 of every device has exactly 1536; group e of device s feeds owner s + e - 2, and is empty where that owner does not exist; each of the 2048 fine rows of a device is named exactly once. `recv_row`: entry (o * 5 + e) * 1536 + j is live exactly where send_row entry (s * 5 + e) * 1536 + j is, with s = o - e + 2.
All inputs are finite; a program needn't handle non-finite values.
Results may differ from a plain program's by a relative error of at most 0.0047.
Values may be sent and summed in bfloat16 or wider, within the bound.
A program may use at most 64 MiB of HBM per device.

v0:
```python
import jax
import jax.numpy as jnp
from jax import lax
from jax.sharding import PartitionSpec as P

REACH = 2
SPAN = 5
CAP = 1536
COARSE = 1024


EPSILON = 1e-05


def from_behind(block, axis, distance):
    devices = range(lax.axis_size(axis))
    route = [(i - distance, i) for i in devices if i - distance in devices]
    return lax.ppermute(block, axis, route)


def shards(fine_feat, conv_weight, norm_gain, norm_bias, send_row, recv_row):
    width_part = conv_weight.shape[1]
    channel_sum = jnp.einsum(
        "koc,kcf->okf",
        conv_weight,
        lax.all_gather(fine_feat, "ch", axis=1, tiled=True),
        preferred_element_type=jnp.float32,
    )
    contribution = channel_sum.astype(jnp.bfloat16).reshape(width_part, -1)
    send_table = send_row.reshape(SPAN, CAP)
    chosen = jnp.take(contribution, jnp.maximum(send_row, 0), axis=1).reshape(width_part, SPAN, CAP)
    outgoing = jnp.where((send_table >= 0)[None, :, :], chosen, jnp.zeros((), jnp.bfloat16))
    pieces = []
    for group in range(SPAN):
        if group == REACH:
            pieces.append(outgoing[:, group])
        else:
            pieces.append(from_behind(outgoing[:, group], "vox", group - REACH))
    incoming = jnp.stack(pieces, axis=1)
    coarse_ids = jnp.arange(COARSE, dtype=jnp.int32)[None, :]
    onehot = (recv_row[:, None] == coarse_ids).astype(jnp.bfloat16)
    coarse = jnp.dot(
        incoming.reshape(width_part, SPAN * CAP), onehot, preferred_element_type=jnp.float32
    )
    hits = jnp.sum(onehot.astype(jnp.float32), axis=0)
    live = (hits > 0).astype(jnp.float32)[None, :]
    total, number = lax.psum((jnp.sum(coarse * live, 1), jnp.sum(live)), "vox")
    mean = (total / number)[:, None]
    centred = (coarse - mean) * live
    spread_sum = lax.psum(jnp.sum(centred * centred, 1), "vox")
    var = (spread_sum / number)[:, None]
    result = (
        jnp.maximum(
            (coarse - mean) * lax.rsqrt(var + EPSILON) * norm_gain[:, None] + norm_bias[:, None],
            0.0,
        )
        * live
    )
    return result.astype(jnp.bfloat16)


def solution(mesh):
    in_specs = (P("vox", "ch", None), P(None, "ch", None), P("ch"), P("ch"), P("vox"), P("vox"))
    out_specs = P("ch", "vox")
    return jax.shard_map(shards, mesh=mesh, in_specs=in_specs, out_specs=out_specs, check_vma=False)
```

profile of v0, /device:TPU:1, one launch (start us, length us, event | category | flops | bytes accessed | tf_op | source)
XLA Modules:
  0.0 611.3 jit_solution(17248120876411528355)
XLA Ops:
  6.5 0.0 copy-start
  6.5 0.0 all-gather.2.cloned.1.call-start
  6.5 0.7 all-gather.2.cloned.1.call-update
  7.3 0.8 broadcast_compare_fusion.1
  8.1 0.8 broadcast_maximum_fusion
  8.9 34.5 %all-gather.2.cloned.1.call-done = bf16[8,256,256]{2,1,0:T(8,128)(2,1)} async-done(((bf16[8,64,256]{2,1,0:T(8,128)(2,1)}), bf16[8,256,256]{2,1,0:T(8,128)(2,1)}) %all-gather.2.cloned.1.call-update) | async-done | bytes 1048592 | tf_op jit(solution)/shard_map/all_gather | solution.py:26
  43.4 0.0 copy-done
  43.4 1.5 fusion.3
  44.9 0.3 copy.11
  45.2 14.4 %gather_fusion = bf16[7680,64]{1,0:T(8,128)(2,1)S(1)} fusion(bf16[64,2048]{0,1:T(8,128)(2,1)S(1)} %bitcast.26, s32[8192]{0:T(1024)S(1)} %pad_clamp_fusion), kind=kCustom, calls=%fused_computation | custom fusion | bytes 1996800 | tf_op jit(solution)/shard_map/jit(_take)/gather | solution.py:31
  59.6 0.0 copy-start.3
  59.6 3.0 select_select_fusion
  62.5 0.1 slice_bitcast_fusion.2
  62.6 1.3 collective-permute-start
  63.9 0.0 copy-done.3
  63.9 4.2 convert_reduce_fusion
  68.1 0.6 fusion.4
  68.7 3.5 collective-permute-start.1
  72.2 1.3 collective-permute-done
  73.5 6.3 %collective-permute-done.1 = bf16[64,1536]{0,1:T(8,128)(2,1)S(1)} collective-permute-done((bf16[64,1536]{0,1:T(8,128)(2,1)S(1)}, bf16[64,1536]{0,1:T(8,128)(2,1)S(1)}, u32[]{:S(2)}, u32[]{:S(2)}) %collective-permute-start.1) | collective-permute-done | bytes 196640 | tf_op jit(solution)/shard_map/ppermute | solution.py:18
  79.9 0.1 bitcast_dynamic-update-slice_fusion.2
  79.9 0.1 slice_bitcast_fusion
  80.0 1.9 collective-permute-start.2
  82.0 3.3 collective-permute-start.3
  85.3 1.4 collective-permute-done.2
  86.7 0.1 bitcast_dynamic-update-slice_fusion.1
  86.7 8.3 %collective-permute-done.3 = bf16[64,1536]{0,1:T(8,128)(2,1)S(1)} collective-permute-done((bf16[64,1536]{0,1:T(8,128)(2,1)S(1)}, bf16[64,1536]{0,1:T(8,128)(2,1)S(1)}, u32[]{:S(2)}, u32[]{:S(2)}) %collective-permute-start.3) | collective-permute-done | bytes 196640 | tf_op jit(solution)/shard_map/ppermute | solution.py:18
  95.0 0.1 bitcast_dynamic-update-slice_fusion
  95.1 0.0 copy-start.1
  95.1 0.0 copy-start.2
  95.1 5.6 multiply_reduce_fusion.1
  100.7 249.7 %all-reduce = (f32[64]{0:T(128)S(1)}, f32[]{:T(128)}) all-reduce(f32[64]{0:T(128)S(1)} %get-tuple-element.14, f32[]{:T(128)} %fusion.4), channel_id=1, replica_groups=mesh['vox'=128,'ch'=4] {'vox'}, use_global_device_ids=true, to_apply=%region_2.3 | all-reduce | flops 65 | bytes 520 | tf_op jit(solution)/shard_map/psum | solution.py:47
  350.3 0.6 broadcast_divide_fusion
  351.0 0.2 multiply_reduce_fusion
  351.2 251.8 %psum.23 = f32[64]{0:T(128)S(1)} all-reduce(f32[64]{0:T(128)S(1)} %multiply_reduce_fusion), channel_id=1, replica_groups=mesh['vox'=128,'ch'=4] {'vox'}, use_global_device_ids=true, to_apply=%region_6.7 | all-reduce | flops 64 | bytes 512 | tf_op jit(solution)/shard_map/psum | solution.py:50
  603.0 0.7 add_rsqrt_fusion
  603.7 0.0 copy-done.1
  603.7 0.0 copy-done.2
  603.7 0.8 multiply_convert_fusion
  (5 shorter events, 0.1 us)
Async XLA Ops:
  6.5 36.8 %copy-start = (bf16[8,64,256]{2,1,0:T(8,128)(2,1)S(1)}, bf16[8,64,256]{2,1,0:T(8,128)(2,1)}, u32[]{:S(2)}) copy-start(bf16[8,64,256]{2,1,0:T(8,128)(2,1)} %param.7) | copy-start | bytes 786436
  6.5 36.8 %all-gather.2.cloned.1.call-start = ((), (), s32[]{:S(2)}) async-start(), calls=%async_computation | async-start | bytes 1310720 | tf_op jit(solution)/shard_map/all_gather | solution.py:26
  59.6 4.3 copy-start.3
  62.6 10.9 %collective-permute-start = (bf16[64,1536]{0,1:T(8,128)(2,1)S(1)}, bf16[64,1536]{0,1:T(8,128)(2,1)S(1)}, u32[]{:S(2)}, u32[]{:S(2)}) collective-permute-start(bf16[64,1536]{0,1:T(8,128)(2,1)S(1)} %get-tuple-element.11), channel_id=1, source_target_pairs={{8,0},{12,4},{16,8},{20,12},{24,16},{28,20},{32,24},{36,28},{40,32... | collective-permute-start | bytes 589832 | tf_op jit(solution)/shard_map/ppermute | solution.py:18
  68.7 11.2 %collective-permute-start.1 = (bf16[64,1536]{0,1:T(8,128)(2,1)S(1)}, bf16[64,1536]{0,1:T(8,128)(2,1)S(1)}, u32[]{:S(2)}, u32[]{:S(2)}) collective-permute-start(bf16[64,1536]{0,1:T(8,128)(2,1)S(1)} %get-tuple-element.10), channel_id=1, source_target_pairs={{4,0},{8,4},{12,8},{16,12},{20,16},{24,20},{28,24},{32,28},{36,32}... | collective-permute-start | bytes 589832 | tf_op jit(solution)/shard_map/ppermute | solution.py:18
  80.0 6.6 %collective-permute-start.2 = (bf16[64,1536]{0,1:T(8,128)(2,1)S(1)}, bf16[64,1536]{0,1:T(8,128)(2,1)S(1)}, u32[]{:S(2)}, u32[]{:S(2)}) collective-permute-start(bf16[64,1536]{0,1:T(8,128)(2,1)S(1)} %get-tuple-element.8), channel_id=1, source_target_pairs={{0,4},{4,8},{8,12},{12,16},{16,20},{20,24},{24,28},{28,32},{32,36}... | collective-permute-start | bytes 589832 | tf_op jit(solution)/shard_map/ppermute | solution.py:18
  82.0 13.0 %collective-permute-start.3 = (bf16[64,1536]{0,1:T(8,128)(2,1)S(1)}, bf16[64,1536]{0,1:T(8,128)(2,1)S(1)}, u32[]{:S(2)}, u32[]{:S(2)}) collective-permute-start(bf16[64,1536]{0,1:T(8,128)(2,1)S(1)} %get-tuple-element.7), channel_id=1, source_target_pairs={{0,8},{4,12},{8,16},{12,20},{16,24},{20,28},{24,32},{28,36},{32,40... | collective-permute-start | bytes 589832 | tf_op jit(solution)/shard_map/ppermute | solution.py:18
  95.1 508.6 %copy-start.1 = (f32[64]{0:T(128)S(1)}, f32[64]{0:T(128)}, u32[]{:S(2)}) copy-start(f32[64]{0:T(128)} %param.9) | copy-start | bytes 772
  95.1 508.6 %copy-start.2 = (f32[64]{0:T(128)S(1)}, f32[64]{0:T(128)}, u32[]{:S(2)}) copy-start(f32[64]{0:T(128)} %param.8) | copy-start | bytes 772
Sparse Core Ops, SparseCore 0:
  9.5 33.8 all-gather.1
where the time goes:
time: 612 us; the launch traced here: 611 us
  blocking collectives  501 us (82%)
  waiting for transfers between devices  52.5 us (9%)
  local copies, waits for them, and re-layouts  15.1 us (2%)
  between operations  13.6 us (2%)
  other arithmetic  11.6 us (2%)
  starting transfers between devices  9.99 us (2%)
  matrix products  7.11 us (1%)
    psum x1, blocking collectives, shards(): spread_sum = lax.psum(jnp.sum(centred * centred, 1), 'vox')  252 us
    psum x1, blocking collectives, shards(): total, number = lax.psum((jnp.sum(coarse * live, 1), jnp.sum(live)), 'vox')  250 us
    all_gather x1, waiting for transfers between devices, shards(): lax.all_gather(fine_feat, 'ch', axis=1, tiled=True)  34.5 us
    ppermute x4, waiting for transfers between devices, from_behind(): return lax.ppermute(block, axis, route)  17.3 us
    gather x1, local copies, waits for them, and re-layouts, shards(): jnp.take(contribution, jnp.maximum(send_row, 0), axis=1)  14.4 us
  transfers between devices with their start and end apart: 5, of which 5 were waited for; matrix products, arithmetic and copies ran while one was open for 1% of the time, Pallas kernels for 0%

commit v1 on v0

v1 whole, which is shorter than its diff:
```python
import functools

import jax
import jax.numpy as jnp
from jax import lax
from jax.experimental import pallas as pl
from jax.experimental.pallas import tpu as pltpu
from jax.sharding import PartitionSpec as P

MESH = pl.DeviceIdType.MESH
LANES = 128
OFFS = 8
FK = 256
SPAN = 5
CAP = 1536
COARSE = 1024
FINE = OFFS * FK
SIDE = FINE - CAP
SIDE_ROWS = SIDE // LANES
GROUP_ROWS = CAP // LANES
CHUNKS = 4
PER = OFFS // CHUNKS
EPSILON = 1e-05
BF16 = jnp.bfloat16
F32 = jnp.float32


def iota(shape, axis):
    return lax.broadcasted_iota(jnp.int32, shape, axis)


def onehot(mask):
    return jnp.where(mask, 1.0, 0.0).astype(BF16)


def combine(parts):
    number = sum(p[2:3] for p in parts)
    total = sum(p[0:1] for p in parts)
    mean = total / jnp.maximum(number, 1.0)
    spread = 0.0
    for p in parts:
        gap = p[0:1] / jnp.maximum(p[2:3], 1.0) - mean
        spread = spread + (p[1:2] + p[2:3] * (gap * gap))
    return total, spread, number


def kernel(
    nx, nv, inner,
    feat, weight, gain, bias, send, recv, out,
    feats, weights, send_tab, recv_tab, route, back, side, own, pay, inc, message, stat1, stat2,
    local_sem, gather_send, gather_recv, pay_send, pay_recv, stat_send, stat_recv,
):
    vox = lax.axis_index("vox")
    ch = lax.axis_index("ch")
    part = feat.shape[1]
    width = weight.shape[1]
    base = (vox // inner) * inner
    place = vox - base
    outer = nv // inner

    x_peer = [lax.rem(ch + d, nx) for d in range(nx)]
    ahead = lambda d: lax.rem(vox + d + nv, nv)
    near = [base + lax.rem(place + d, inner) for d in range(inner)]
    far = [lax.rem(vox + inner * d, nv) for d in range(outer)]

    loads = [
        pltpu.make_async_copy(send, send_tab, local_sem.at[0]),
        pltpu.make_async_copy(recv, recv_tab, local_sem.at[1]),
        pltpu.make_async_copy(weight, weights, local_sem.at[2]),
        pltpu.make_async_copy(feat, feats.at[:, pl.ds(pl.multiple_of(ch * part, part), part)], local_sem.at[3]),
    ]
    for load in loads:
        load.start()

    barrier = pltpu.get_barrier_semaphore()
    greeted = 0
    for peer in x_peer[1:]:
        pl.semaphore_signal(barrier, inc=1, device_id={"ch": peer}, device_id_type=MESH)
        greeted += 1
    for peer in [ahead(-2), ahead(-1), ahead(1), ahead(2)] + near[1:] + far[1:]:
        pl.semaphore_signal(barrier, inc=1, device_id={"vox": peer}, device_id_type=MESH)
        greeted += 1
    pl.semaphore_wait(barrier, greeted)

    def gather_copy(d, chunk, source):
        rows = pl.ds(pl.multiple_of(source * part, part), part)
        return pltpu.make_async_remote_copy(
            src_ref=feat.at[pl.ds(chunk * PER, PER)],
            dst_ref=feats.at[pl.ds(chunk * PER, PER), rows],
            send_sem=gather_send.at[d - 1, chunk],
            recv_sem=gather_recv.at[d - 1, chunk],
            device_id={"ch": x_peer[d]},
            device_id_type=MESH,
        )

    for chunk in range(CHUNKS):
        for d in range(1, nx):
            gather_copy(d, chunk, ch).start()

    loads[0].wait()
    loads[1].wait()
    tables = [[tab[e * GROUP_ROWS : e * GROUP_ROWS + SIDE_ROWS] for e in range(SPAN)] for tab in (send_tab, recv_tab)]
    mirror = onehot(iota((LANES, LANES), 0) + iota((LANES, LANES), 1) == LANES - 1)
    plain = jnp.concatenate([tables[0][3], tables[0][4], tables[1][3], tables[1][4]], axis=0) + 1
    digits = jnp.concatenate([plain // 256, plain % 256], axis=0).astype(F32).astype(BF16)
    turned = jnp.dot(digits, mirror, preferred_element_type=F32)
    turned = turned[: 4 * SIDE_ROWS] * 256.0 + turned[4 * SIDE_ROWS :] - 1.0

    def turned_row(which, b):
        row = which * SIDE_ROWS + SIDE_ROWS - 1 - b
        return turned[row : row + 1]

    named = []
    for left, which in ((0, 1), (1, 0)):
        for b in range(SIDE_ROWS):
            named.append(jnp.maximum(tables[0][left][b : b + 1].astype(F32), turned_row(which, b)))

    owner_send = send_tab[2 * GROUP_ROWS : 3 * GROUP_ROWS].astype(F32)
    owner_recv = recv_tab[2 * GROUP_ROWS : 3 * GROUP_ROWS].astype(F32)
    coarse_ids = iota((LANES, COARSE), 1).astype(F32)

    def route_block(block, carry):
        rows = pl.ds(pl.multiple_of(block * LANES, LANES), LANES)
        fine = (iota((LANES, LANES), 0) + block * LANES).astype(F32)
        for b, names in enumerate(named):
            route[rows, b * LANES : (b + 1) * LANES] = onehot(names == fine)
        target = jnp.full((LANES, LANES), -1.0, F32)
        for b in range(GROUP_ROWS):
            target = jnp.maximum(target, jnp.where(owner_send[b : b + 1] == fine, owner_recv[b : b + 1], -1.0))
        target = jnp.max(target, axis=1, keepdims=True)
        route[rows, 2 * SIDE :] = onehot(target == coarse_ids)
        return carry

    lax.fori_loop(0, FINE // LANES, route_block, 0)

    lists = [tables[1][0].astype(F32), tables[1][1].astype(F32)]
    for which in (2, 3):
        lists.append(jnp.concatenate([turned_row(which, b) for b in range(SIDE_ROWS)], axis=0))
    count = 4 * SIDE_ROWS
    columns = jnp.concatenate(lists + [jnp.zeros((LANES - count, LANES), F32)], axis=0).T
    for b in range(count):
        back[b * LANES : (b + 1) * LANES] = onehot(columns[:, b : b + 1] == coarse_ids)

    ones = jnp.ones((16, FINE), BF16)
    hits = jnp.dot(ones, route[:, 2 * SIDE :], preferred_element_type=F32)
    hits = hits + jnp.dot(ones[:, : 4 * SIDE], back[...], preferred_element_type=F32)
    live = jnp.where(hits[0:1] > 0.0, 1.0, 0.0)
    number = jnp.sum(live, axis=1, keepdims=True)

    loads[2].wait()
    loads[3].wait()

    def contribution(chunk):
        for d in range(1, nx):
            gather_copy(d, chunk, x_peer[nx - d]).wait_recv()
        made = []
        for i in range(PER):
            k = chunk * PER + i
            made.append(jnp.dot(weights[k], feats[k], preferred_element_type=F32).astype(BF16))
        return jnp.concatenate(made, axis=1)

    side[...] = jnp.zeros_like(side)
    own[...] = jnp.zeros_like(own)
    for chunk in range(CHUNKS):
        made = contribution(chunk)
        rows = slice(chunk * PER * FK, (chunk + 1) * PER * FK)
        side[...] += jnp.dot(made, route[rows, : 2 * SIDE], preferred_element_type=F32)
        if chunk == CHUNKS - 1:
            pay[0] = side[:, :SIDE].astype(BF16)
            pay[1] = side[:, SIDE:].astype(BF16)
            moves = []
            for slot, (half, distance) in enumerate(((0, -2), (1, -1), (1, 1), (0, 2))):
                moves.append(
                    pltpu.make_async_remote_copy(
                        src_ref=pay.at[half],
                        dst_ref=inc.at[slot],
                        send_sem=pay_send.at[slot],
                        recv_sem=pay_recv.at[slot],
                        device_id={"vox": ahead(distance)},
                        device_id_type=MESH,
                    )
                )
                moves[-1].start()
        own[...] += jnp.dot(made, route[rows, 2 * SIDE :], preferred_element_type=F32)

    for slot in (1, 2, 0, 3):
        moves[slot].wait_recv()
        own[...] += jnp.dot(inc[slot], back[slot * SIDE : (slot + 1) * SIDE], preferred_element_type=F32)

    coarse = own[...]
    total = jnp.sum(coarse * live, axis=1, keepdims=True)
    centred = (coarse - total / jnp.maximum(number, 1.0)) * live
    spread = jnp.sum(centred * centred, axis=1, keepdims=True)
    lane = iota((width, LANES), 1)
    table = jnp.where(lane == 0, total, jnp.where(lane == 1, spread, jnp.where(lane == 2, number, 0.0)))
    table = jnp.concatenate([table, jnp.zeros((LANES - width, LANES), F32)], axis=0).T
    message[0] = table[:4]

    def share(step, peers, held):
        for d in range(1, len(peers)):
            pltpu.make_async_remote_copy(
                src_ref=message.at[step],
                dst_ref=held.at[d - 1],
                send_sem=stat_send.at[step],
                recv_sem=stat_recv.at[step],
                device_id={"vox": peers[d]},
                device_id_type=MESH,
            ).start()
        pltpu.make_async_copy(held, held, stat_recv.at[step]).wait()
        return combine([message[step]] + [held[d] for d in range(len(peers) - 1)])

    total, spread, number = share(0, near, stat1)
    message[1] = jnp.concatenate([total, spread, number, jnp.zeros_like(total)], axis=0)
    total, spread, number = share(1, far, stat2)

    number = jnp.maximum(number, 1.0)
    mean = total / number
    scale = lax.rsqrt(spread / number + EPSILON)[:, :width] * gain[...]
    rows = jnp.concatenate([mean[:, :width], scale, bias[...], jnp.zeros((5, width), F32)], axis=0)
    rows = jnp.concatenate([rows, jnp.zeros((8, LANES - width), F32)], axis=1)
    rows = jnp.concatenate([rows, jnp.zeros((LANES - 8, LANES), F32)], axis=0).T
    mean, scale, shift = (rows[:width, i : i + 1] for i in range(3))
    out[...] = (jnp.maximum((coarse - mean) * scale + shift, 0.0) * live).astype(out.dtype)

    for chunk in range(CHUNKS):
        for d in range(1, nx):
            gather_copy(d, chunk, ch).wait_send()
    for move in moves:
        move.wait_send()
    pltpu.make_async_copy(stat1, stat1, stat_send.at[0]).wait()
    pltpu.make_async_copy(stat2, stat2, stat_send.at[1]).wait()


def solution(mesh, inner=16):
    nx, nv = mesh.shape["ch"], mesh.shape["vox"]

    def shards(fine_feat, conv_weight, norm_gain, norm_bias, send_row, recv_row):
        width = conv_weight.shape[1]
        channels = conv_weight.shape[2]
        anywhere = pl.BlockSpec(memory_space=pl.ANY)
        vmem = pl.BlockSpec(memory_space=pltpu.VMEM)
        table = (SPAN * GROUP_ROWS, LANES)
        return pl.pallas_call(
            functools.partial(kernel, nx, nv, inner),
            out_shape=jax.ShapeDtypeStruct((width, COARSE), BF16),
            in_specs=[anywhere, anywhere, vmem, vmem, anywhere, anywhere],
            out_specs=vmem,
            scratch_shapes=[
                pltpu.VMEM((OFFS, channels, FK), BF16),
                pltpu.VMEM((OFFS, width, channels), BF16),
                pltpu.VMEM(table, jnp.int32),
                pltpu.VMEM(table, jnp.int32),
                pltpu.VMEM((FINE, 2 * SIDE + COARSE), BF16),
                pltpu.VMEM((4 * SIDE, COARSE), BF16),
                pltpu.VMEM((width, 2 * SIDE), F32),
                pltpu.VMEM((width, COARSE), F32),
                pltpu.VMEM((2, width, SIDE), BF16),
                pltpu.VMEM((4, width, SIDE), BF16),
                pltpu.VMEM((2, 4, LANES), F32),
                pltpu.VMEM((inner - 1, 4, LANES), F32),
                pltpu.VMEM((nv // inner - 1, 4, LANES), F32),
                pltpu.SemaphoreType.DMA((4,)),
                pltpu.SemaphoreType.DMA((nx - 1, CHUNKS)),
                pltpu.SemaphoreType.DMA((nx - 1, CHUNKS)),
                pltpu.SemaphoreType.DMA((4,)),
                pltpu.SemaphoreType.DMA((4,)),
                pltpu.SemaphoreType.DMA((2,)),
                pltpu.SemaphoreType.DMA((2,)),
            ],
            compiler_params=pltpu.CompilerParams(
                collective_id=0, has_side_effects=True, vmem_limit_bytes=48 * 1024 * 1024
            ),
        )(
            fine_feat,
            conv_weight,
            norm_gain.reshape(1, width),
            norm_bias.reshape(1, width),
            send_row.reshape(table),
            recv_row.reshape(table),
        )

    in_specs = (P("vox", "ch", None), P(None, "ch", None), P("ch"), P("ch"), P("vox"), P("vox"))
    out_specs = P("ch", "vox")
    return jax.shard_map(shards, mesh=mesh, in_specs=in_specs, out_specs=out_specs, check_vma=False)
```

time: 612 us -> 50.1 us (0.08)
  blocking collectives: 501 us -> 0 us
  waiting for transfers between devices: 52.5 us -> 0 us
  Pallas kernels: 0 us -> 45 us
  between operations: 13.6 us -> 0.02 us
  other arithmetic: 11.6 us -> 0 us
  local copies, waits for them, and re-layouts: 15.1 us -> 4.74 us
  starting transfers between devices: 9.99 us -> 0 us
  matrix products: 7.11 us -> 0 us
    psum x2 -> x0, blocking collectives: 501 us -> none  [the longest x1 252 us: shards(): spread_sum = lax.psum(jnp.sum(centred * centred, 1), 'vox')]
    pallas_call x0 -> x1, Pallas kernels: none -> 45 us  [shards(): pl.pallas_call(functools.partial(kernel, nx, nv, inner), out_shape=jax.Sh...]
    all_gather x1 -> x0, waiting for transfers between devices: 34.5 us -> none  [shards(): lax.all_gather(fine_feat, 'ch', axis=1, tiled=True)]
    ppermute x4 -> x0, waiting for transfers between devices: 17.3 us -> none  [from_behind(): return lax.ppermute(block, axis, route)]
    gather x1 -> x0, local copies, waits for them, and re-layouts: 14.4 us -> none  [shards(): jnp.take(contribution, jnp.maximum(send_row, 0), axis=1)]
    ppermute x4 -> x0, starting transfers between devices: 9.98 us -> none  [from_behind(): return lax.ppermute(block, axis, route)]
    dot_general x2 -> x0, matrix products: 7.11 us -> none  [the longest x1 5.59 us: shards(): jnp.dot(incoming.reshape(width_part, SPAN * CAP), onehot, preferred_eleme...]
  transfers between devices with their start and end apart: 5 -> 0, of which waited for: 5 -> 0; matrix products, arithmetic and copies ran while one was open for 1% -> 0% of each run, Pallas kernels for 0% -> 0%
where the time goes in v1:
time: 50.1 us; the launch traced here: 49.8 us
  Pallas kernels  45 us (90%)
  local copies, waits for them, and re-layouts  4.74 us (9%)
    pallas_call x1, Pallas kernels, shards(): pl.pallas_call(functools.partial(kernel, nx, nv, inner), out_shape=jax.Sh...  45 us
    unnamed x13, local copies, waits for them, and re-layouts  4.74 us

profile of v1, /device:TPU:1, one launch (start us, length us, event | category | flops | bytes accessed | tf_op | source)
XLA Modules:
  0.0 49.8 jit_solution(18431608834485157644)
XLA Ops:
  0.0 0.0 copy-start.4
  0.0 0.0 copy-start.5
  0.0 0.7 %copy-done.4 = f32[64]{0:T(128)S(1)} copy-done((f32[64]{0:T(128)S(1)}, f32[64]{0:T(128)}, u32[]{:S(2)}) %copy-start.4) | copy-done | bytes 280
  0.7 0.0 copy-done.5
  0.7 0.0 copy-start
  0.7 0.9 %copy-done = bf16[8,64,256]{2,1,0:T(8,128)(2,1)S(1)} copy-done((bf16[8,64,256]{2,1,0:T(8,128)(2,1)S(1)}, bf16[8,64,256]{2,1,0:T(8,128)(2,1)}, u32[]{:S(2)}) %copy-start) | copy-done | bytes 262168
  1.6 0.0 copy-start.1
  1.6 0.9 %copy-done.1 = bf16[8,64,256]{2,1,0:T(8,128)(2,1)S(1)} copy-done((bf16[8,64,256]{2,1,0:T(8,128)(2,1)S(1)}, bf16[8,64,256]{2,1,0:T(8,128)(2,1)}, u32[]{:S(2)}) %copy-start.1) | copy-done | bytes 262168
  2.6 0.0 copy-start.2
  2.6 0.8 %copy-done.2 = s32[7680]{0:T(1024)S(1)} copy-done((s32[7680]{0:T(1024)S(1)}, s32[7680]{0:T(1024)}, u32[]{:S(2)}) %copy-start.2) | copy-done | bytes 30744
  3.3 0.0 copy-start.3
  3.3 0.8 %copy-done.3 = s32[7680]{0:T(1024)S(1)} copy-done((s32[7680]{0:T(1024)S(1)}, s32[7680]{0:T(1024)}, u32[]{:S(2)}) %copy-start.3) | copy-done | bytes 30744
  4.1 45.0 %shard_map.64 = bf16[64,1024]{1,0:T(8,128)(2,1)S(1)} custom-call(bf16[8,64,256]{2,1,0:T(8,128)(2,1)S(1)} %copy-done, bf16[8,64,256]{2,1,0:T(8,128)(2,1)S(1)} %copy-done.1, f32[1,64]{1,0:T(1,128)S(1)} %bitcast.6, f32[1,64]{1,0:T(1,128)S(1)} %bitcast.7, s32[60,128]{1,0:T(8,128)S(1)} %bitcast.4, s32[60,128]{1,0:T(8,128)S(1)} %bitcast.5), custom_call_target="tpu_custom_call" | custom-call | tf_op jit(solution)/shard_map/pallas_call | solution.py:243
  49.1 0.7 %copy.8 = bf16[64,1024]{1,0:T(8,128)(2,1)} copy(bf16[64,1024]{1,0:T(8,128)(2,1)S(1)} %shard_map.64) | data formatting | bytes 262144
Async XLA Ops:
  0.0 0.7 %copy-start.4 = (f32[64]{0:T(128)S(1)}, f32[64]{0:T(128)}, u32[]{:S(2)}) copy-start(f32[64]{0:T(128)} %param.8) | copy-start | bytes 772
  0.0 0.7 %copy-start.5 = (f32[64]{0:T(128)S(1)}, f32[64]{0:T(128)}, u32[]{:S(2)}) copy-start(f32[64]{0:T(128)} %param.9) | copy-start | bytes 772
  0.7 0.9 %copy-start = (bf16[8,64,256]{2,1,0:T(8,128)(2,1)S(1)}, bf16[8,64,256]{2,1,0:T(8,128)(2,1)}, u32[]{:S(2)}) copy-start(bf16[8,64,256]{2,1,0:T(8,128)(2,1)} %feat.1) | copy-start | bytes 786436
  1.6 0.9 %copy-start.1 = (bf16[8,64,256]{2,1,0:T(8,128)(2,1)S(1)}, bf16[8,64,256]{2,1,0:T(8,128)(2,1)}, u32[]{:S(2)}) copy-start(bf16[8,64,256]{2,1,0:T(8,128)(2,1)} %weight.1) | copy-start | bytes 786436
  2.6 0.8 %copy-start.2 = (s32[7680]{0:T(1024)S(1)}, s32[7680]{0:T(1024)}, u32[]{:S(2)}) copy-start(s32[7680]{0:T(1024)} %param.10) | copy-start | bytes 92164
  3.3 0.8 %copy-start.3 = (s32[7680]{0:T(1024)S(1)}, s32[7680]{0:T(1024)}, u32[]{:S(2)}) copy-start(s32[7680]{0:T(1024)} %param.11) | copy-start | bytes 92164

commit v2 on v0

v2 whole, which is shorter than its diff:
```python
import functools

import jax
import jax.numpy as jnp
from jax import lax
from jax.experimental import pallas as pl
from jax.experimental.pallas import tpu as pltpu
from jax.sharding import PartitionSpec as P

MESH = pl.DeviceIdType.MESH
LANES = 128
OFFS = 8
FK = 256
SPAN = 5
CAP = 1536
COARSE = 1024
SIDE = OFFS * FK - CAP
SIDE_ROWS = SIDE // LANES
GROUP_ROWS = CAP // LANES
PACKS = OFFS * FK // SIDE
EPSILON = 1e-05
BF16 = jnp.bfloat16
F32 = jnp.float32


def iota(shape, axis):
    return lax.broadcasted_iota(jnp.int32, shape, axis)


def onehot(mask):
    return jnp.where(mask, 1.0, 0.0).astype(BF16)


def lanes(rows):
    return jnp.concatenate([rows[b : b + 1] for b in range(rows.shape[0])], axis=1)


def merge(first, second):
    number = first[1:2] + second[1:2]
    gap = first[0:1] / jnp.maximum(first[1:2], 1.0) - second[0:1] / jnp.maximum(second[1:2], 1.0)
    gap = gap * gap * (first[1:2] * second[1:2] / jnp.maximum(number, 1.0))
    lane = iota(gap.shape, 1)
    gap = jnp.where(lane < LANES // 2, 0.0, pltpu.roll(gap, LANES // 2, 1))
    return jnp.concatenate([first[0:1] + second[0:1] + gap, number], axis=0)


def kernel(
    ny, nz,
    feat, weight, gain, bias, send, recv, out,
    local, packs, weights, gain_row, bias_row, send_tab, recv_tab, back, own, pay, inc, message, pair, held,
    local_sem, side_send, side_recv, own_send, own_recv, pay_send, pay_recv, stat_send, stat_recv,
):
    vox = lax.axis_index("vox")
    ch = lax.axis_index("ch")
    nx = 4
    nv = ny * nz * 2
    part = feat.shape[1]
    width = weight.shape[1]
    core, z, y = vox % 2, (vox // 2) % nz, vox // (2 * nz)

    x_peer = [lax.rem(ch + d, nx) for d in range(nx)]
    ahead = {d: lax.rem(vox + d + nv, nv) for d in (-2, -1, 1, 2)}
    sibling = vox + 1 - 2 * core
    steps = [(min(a, ny - a) + min(b, nz - b), a, b) for a in range(ny) for b in range(nz)]
    steps = sorted(steps, reverse=True)[:-1]
    chips = [(lax.rem(y + a, ny) * nz + lax.rem(z + b, nz)) * 2 + core for _, a, b in steps]

    def rows_of(source, first=0, size=part):
        return pl.ds(pl.multiple_of(source * part + first, 16), size)

    loads = [
        pltpu.make_async_copy(src, dst, local_sem.at[i])
        for i, (src, dst) in enumerate(
            ((send, send_tab), (feat, local), (recv, recv_tab), (weight, weights), (gain, gain_row), (bias, bias_row))
        )
    ]
    for load in loads:
        load.start()

    barrier = pltpu.get_barrier_semaphore()
    for peer in x_peer[1:]:
        pl.semaphore_signal(barrier, inc=1, device_id={"ch": peer}, device_id_type=MESH)
    greeted = list(ahead.values()) + [sibling] + chips
    for peer in greeted:
        pl.semaphore_signal(barrier, inc=1, device_id={"vox": peer}, device_id_type=MESH)

    loads[0].wait()
    side_ids = (0, 1, 3, 4)
    lists = {e: send_tab[e * GROUP_ROWS : e * GROUP_ROWS + SIDE_ROWS] for e in side_ids}
    counts, starts, start = {}, {}, jnp.zeros((1, 1), F32)
    for e in side_ids:
        alive = jnp.where(lists[e] >= 0, 1.0, 0.0)
        counts[e] = jnp.sum(jnp.sum(alive, axis=1, keepdims=True), axis=0, keepdims=True)
        starts[e] = start
        start = start + counts[e]
    shift = (iota((SIDE, SIDE), 1) - iota((SIDE, SIDE), 0)).astype(F32)
    packed = jnp.zeros((16, SIDE), F32)
    for e in side_ids:
        value = lanes(lists[e]) + 1
        digits = jnp.where(iota((16, SIDE), 0) == 0, value >> 8, value & 255).astype(F32).astype(BF16)
        packed = packed + jnp.dot(digits, onehot(shift == starts[e]), preferred_element_type=F32)
    names = [packed[0:1] * 256.0 + packed[1:2] - 1.0]
    mine = send_tab[2 * GROUP_ROWS : 3 * GROUP_ROWS].astype(F32)
    for i in range(PACKS - 1):
        names.append(lanes(mine[i * SIDE_ROWS : (i + 1) * SIDE_ROWS]))

    def pack(i):
        total = jnp.zeros((part, SIDE), F32)
        for k in range(OFFS):
            fine = (iota((FK, SIDE), 0) + k * FK).astype(F32)
            total = total + jnp.dot(local[k], onehot(names[i] == fine), preferred_element_type=F32)
        packs[i, rows_of(ch), :] = total.astype(BF16)

    def side_copy(d, source):
        block = packs.at[0, rows_of(source)]
        return pltpu.make_async_remote_copy(
            src_ref=block, dst_ref=block, send_sem=side_send.at[d - 1], recv_sem=side_recv.at[d - 1],
            device_id={"ch": x_peer[d]}, device_id_type=MESH,
        )

    def own_copy(i, way, source, first=0, size=part):
        block = packs.at[i, rows_of(source, first, size)]
        return pltpu.make_async_remote_copy(
            src_ref=block, dst_ref=block, send_sem=own_send.at[way, i - 1], recv_sem=own_recv.at[way, i - 1],
            device_id={"ch": x_peer[1 if way % 2 == 0 else nx - 1]}, device_id_type=MESH,
        )

    half = part // 2
    loads[1].wait()
    pack(0)
    pl.semaphore_wait(barrier, nx - 1 + len(greeted))
    for d in (2, 1, 3):
        side_copy(d, ch).start()
    for i in range(1, PACKS):
        pack(i)
        own_copy(i, 0, ch).start()
        own_copy(i, 1, ch).start()

    place = iota((1, SIDE), 1).astype(F32)
    mirrored = SIDE - 1.0 - place
    sources = []
    for left, right in ((0, 4), (1, 3)):
        tail = jnp.where(mirrored < counts[right], starts[right] + mirrored, -1.0)
        sources.append(jnp.where(place < counts[left], starts[left] + place, tail))
    column = iota((SIDE, SIDE), 0).astype(F32)
    spread_out = [onehot(source == column) for source in sources]

    loads[2].wait()
    mirror = onehot(iota((LANES, LANES), 0) + iota((LANES, LANES), 1) == LANES - 1)
    turned = jnp.concatenate([recv_tab[e * GROUP_ROWS : e * GROUP_ROWS + SIDE_ROWS] for e in (3, 4)], axis=0) + 1
    digits = jnp.concatenate([turned >> 8, turned & 255], axis=0).astype(F32).astype(BF16)
    turned = jnp.dot(digits, mirror, preferred_element_type=F32)
    turned = turned[: 2 * SIDE_ROWS] * 256.0 + turned[2 * SIDE_ROWS :] - 1.0
    targets = [recv_tab[2 * GROUP_ROWS : 3 * GROUP_ROWS].astype(F32)]
    for e in (0, 1):
        targets.append(recv_tab[e * GROUP_ROWS : e * GROUP_ROWS + SIDE_ROWS].astype(F32))
    for e in (0, 1):
        targets += [turned[(e + 1) * SIDE_ROWS - 1 - b : (e + 1) * SIDE_ROWS - b] for b in range(SIDE_ROWS)]
    blocks = GROUP_ROWS + 4 * SIDE_ROWS
    targets = jnp.concatenate(targets + [jnp.zeros((LANES - blocks, LANES), F32)], axis=0).T
    coarse_ids = iota((LANES, COARSE), 1).astype(F32)
    hits = jnp.zeros((8, COARSE), F32)

    def fill(first, last, hits):
        for b in range(first, last):
            found = jnp.where(targets[:, b : b + 1] == coarse_ids, 1.0, 0.0)
            back[b * LANES : (b + 1) * LANES] = found.astype(BF16)
            hits = hits + jnp.sum(found.reshape(LANES // 8, 8, COARSE), axis=0)
        return hits

    def convolve(i):
        every = jnp.dot(weights[...].reshape(OFFS * width, -1), packs[i], preferred_element_type=F32)
        chosen = every[:width]
        for k in range(1, OFFS):
            chosen = jnp.where(names[i] >= float(k * FK), every[k * width : (k + 1) * width], chosen)
        return chosen.astype(BF16)

    def pass_on(i):
        own_copy(i, 0, x_peer[nx - 1]).wait_recv()
        own_copy(i, 2, x_peer[nx - 1], 0, half).start()
        own_copy(i, 1, x_peer[1]).wait_recv()
        own_copy(i, 3, x_peer[1], half, half).start()

    hits = fill(0, GROUP_ROWS, hits)
    loads[3].wait()
    for d in range(1, nx):
        side_copy(d, x_peer[nx - d]).wait_recv()
    made = convolve(0)
    moves = []
    for part_of, which in ((0, ((0, -2), (3, 2))), (1, ((1, -1), (2, 1)))):
        pay[part_of] = jnp.dot(made, spread_out[part_of], preferred_element_type=F32).astype(BF16)
        for slot, distance in which:
            moves.append(
                pltpu.make_async_remote_copy(
                    src_ref=pay.at[part_of], dst_ref=inc.at[slot],
                    send_sem=pay_send.at[slot], recv_sem=pay_recv.at[slot],
                    device_id={"vox": ahead[distance]}, device_id_type=MESH,
                )
            )
            moves[-1].start()
    pass_on(1)
    hits = fill(GROUP_ROWS, blocks, hits)
    pass_on(2)
    pass_on(3)
    live = jnp.where(jnp.sum(hits, axis=0, keepdims=True) > 0.0, 1.0, 0.0)
    number = jnp.sum(live, axis=1, keepdims=True)

    for i in range(1, PACKS):
        own_copy(i, 2, x_peer[2], 0, half).wait_recv()
        own_copy(i, 3, x_peer[2], half, half).wait_recv()
        sums = jnp.dot(convolve(i), back[(i - 1) * SIDE : i * SIDE], preferred_element_type=F32)
        own[...] = sums if i == 1 else own[...] + sums
    for move, slot in zip(moves, (0, 3, 1, 2)):
        move.wait_recv()
    base = GROUP_ROWS * LANES
    for slot in (0, 1, 3, 2):
        matrix = back[base + slot * SIDE : base + (slot + 1) * SIDE]
        own[...] += jnp.dot(inc[slot], matrix, preferred_element_type=F32)

    coarse = own[...]
    total = jnp.sum(coarse * live, axis=1, keepdims=True)
    centred = (coarse - total / jnp.maximum(number, 1.0)) * live
    spread = jnp.sum(centred * centred, axis=1, keepdims=True)
    column = jnp.concatenate([total, spread], axis=0)
    message[0] = jnp.concatenate(
        [jnp.broadcast_to(column, (LANES, LANES)).T[0:1], jnp.broadcast_to(number, (1, LANES))], axis=0
    )
    swap = pltpu.make_async_remote_copy(
        src_ref=message.at[0], dst_ref=pair, send_sem=stat_send.at[0], recv_sem=stat_recv.at[0],
        device_id={"vox": sibling}, device_id_type=MESH,
    )
    swap.start()
    swap.wait_recv()
    message[1] = merge(message[0], pair[...])
    for j, peer in enumerate(chips):
        pltpu.make_async_remote_copy(
            src_ref=message.at[1], dst_ref=held.at[j], send_sem=stat_send.at[1], recv_sem=stat_recv.at[1],
            device_id={"vox": peer}, device_id_type=MESH,
        ).start()
    pltpu.make_async_copy(held, held, stat_recv.at[1]).wait()

    parts = [message[1]] + [held[j] for j in range(len(chips))]
    sums = sum(parts)
    number = jnp.maximum(sums[1:2], 1.0)
    mean = sums[0:1] / number
    gaps = jnp.zeros((1, LANES), F32)
    for p in parts:
        gap = p[0:1] / jnp.maximum(p[1:2], 1.0) - mean
        gaps = gaps + gap * gap * p[1:2]
    loads[4].wait()
    loads[5].wait()
    variance = (pltpu.roll(sums[0:1], LANES // 2, 1) + gaps) / number
    scale = lax.rsqrt(variance + EPSILON)[:, :width] * gain_row[...]
    rows = jnp.concatenate([mean[:, :width], scale, bias_row[...], jnp.zeros((5, width), F32)], axis=0)
    rows = jnp.concatenate([rows, jnp.zeros((8, LANES - width), F32)], axis=1)
    rows = jnp.concatenate([rows, jnp.zeros((LANES - 8, LANES), F32)], axis=0).T
    mean, scale, offset = (rows[:width, i : i + 1] for i in range(3))
    out[...] = (jnp.maximum((coarse - mean) * scale + offset, 0.0) * live).astype(out.dtype)

    for d in range(1, nx):
        side_copy(d, ch).wait_send()
    for i in range(1, PACKS):
        own_copy(i, 0, ch).wait_send()
        own_copy(i, 1, ch).wait_send()
        own_copy(i, 2, x_peer[nx - 1], 0, half).wait_send()
        own_copy(i, 3, x_peer[1], half, half).wait_send()
    for move in moves:
        move.wait_send()
    swap.wait_send()
    pltpu.make_async_copy(held, held, stat_send.at[1]).wait()


def solution(mesh, ny=8, nz=8):
    def shards(fine_feat, conv_weight, norm_gain, norm_bias, send_row, recv_row):
        offsets, width, channels = conv_weight.shape
        part = fine_feat.shape[1]
        hbm = pl.BlockSpec(memory_space=pltpu.HBM)
        vmem = pl.BlockSpec(memory_space=pltpu.VMEM)
        table = (SPAN * GROUP_ROWS, LANES)
        return pl.pallas_call(
            functools.partial(kernel, ny, nz),
            out_shape=jax.ShapeDtypeStruct((width, COARSE), BF16),
            in_specs=[hbm] * 6,
            out_specs=vmem,
            scratch_shapes=[
                pltpu.VMEM((offsets, part, FK), BF16),
                pltpu.VMEM((PACKS, channels, SIDE), BF16),
                pltpu.VMEM((offsets, width, channels), BF16),
                pltpu.VMEM((1, width), F32),
                pltpu.VMEM((1, width), F32),
                pltpu.VMEM(table, jnp.int32),
                pltpu.VMEM(table, jnp.int32),
                pltpu.VMEM((CAP + 4 * SIDE, COARSE), BF16),
                pltpu.VMEM((width, COARSE), F32),
                pltpu.VMEM((2, width, SIDE), BF16),
                pltpu.VMEM((4, width, SIDE), BF16),
                pltpu.VMEM((2, 2, LANES), F32),
                pltpu.VMEM((2, LANES), F32),
                pltpu.VMEM((ny * nz - 1, 2, LANES), F32),
                pltpu.SemaphoreType.DMA((6,)),
                pltpu.SemaphoreType.DMA((3,)),
                pltpu.SemaphoreType.DMA((3,)),
                pltpu.SemaphoreType.DMA((4, PACKS - 1)),
                pltpu.SemaphoreType.DMA((4, PACKS - 1)),
                pltpu.SemaphoreType.DMA((4,)),
                pltpu.SemaphoreType.DMA((4,)),
                pltpu.SemaphoreType.DMA((2,)),
                pltpu.SemaphoreType.DMA((2,)),
            ],
            compiler_params=pltpu.CompilerParams(
                collective_id=0, has_side_effects=True, vmem_limit_bytes=60 * 1024 * 1024
            ),
        )(
            fine_feat,
            conv_weight,
            norm_gain.reshape(1, width),
            norm_bias.reshape(1, width),
            send_row.reshape(table),
            recv_row.reshape(table),
        )

    in_specs = (P("vox", "ch", None), P(None, "ch", None), P("ch"), P("ch"), P("vox"), P("vox"))
    out_specs = P("ch", "vox")
    return jax.shard_map(shards, mesh=mesh, in_specs=in_specs, out_specs=out_specs, check_vma=False)
```

time: 612 us -> 40.9 us (0.07)
  blocking collectives: 501 us -> 0 us
  waiting for transfers between devices: 52.5 us -> 0 us
  Pallas kernels: 0 us -> 39.2 us
  between operations: 13.6 us -> 0.01 us
  local copies, waits for them, and re-layouts: 15.1 us -> 1.57 us
  other arithmetic: 11.6 us -> 0 us
  starting transfers between devices: 9.99 us -> 0 us
  matrix products: 7.11 us -> 0 us
    psum x2 -> x0, blocking collectives: 501 us -> none  [the longest x1 252 us: shards(): spread_sum = lax.psum(jnp.sum(centred * centred, 1), 'vox')]
    pallas_call x0 -> x1, Pallas kernels: none -> 39.2 us  [shards(): pl.pallas_call(functools.partial(kernel, ny, nz), out_shape=jax.ShapeDtyp...]
    all_gather x1 -> x0, waiting for transfers between devices: 34.5 us -> none  [shards(): lax.all_gather(fine_feat, 'ch', axis=1, tiled=True)]
    ppermute x4 -> x0, waiting for transfers between devices: 17.3 us -> none  [from_behind(): return lax.ppermute(block, axis, route)]
    gather x1 -> x0, local copies, waits for them, and re-layouts: 14.4 us -> none  [shards(): jnp.take(contribution, jnp.maximum(send_row, 0), axis=1)]
    ppermute x4 -> x0, starting transfers between devices: 9.98 us -> none  [from_behind(): return lax.ppermute(block, axis, route)]
    dot_general x2 -> x0, matrix products: 7.11 us -> none  [the longest x1 5.59 us: shards(): jnp.dot(incoming.reshape(width_part, SPAN * CAP), onehot, preferred_eleme...]
  transfers between devices with their start and end apart: 5 -> 0, of which waited for: 5 -> 0; matrix products, arithmetic and copies ran while one was open for 1% -> 0% of each run, Pallas kernels for 0% -> 0%
where the time goes in v2:
time: 40.9 us; the launch traced here: 40.7 us
  Pallas kernels  39.2 us (96%)
  local copies, waits for them, and re-layouts  1.57 us (4%)
    pallas_call x1, Pallas kernels, shards(): pl.pallas_call(functools.partial(kernel, ny, nz), out_shape=jax.ShapeDtyp...  39.2 us
    unnamed x1, local copies, waits for them, and re-layouts  1.57 us

profile of v2, /device:TPU:1, one launch (start us, length us, event | category | flops | bytes accessed | tf_op | source)
XLA Modules:
  0.0 40.7 jit_solution(18226006793630111975)
XLA Ops:
  0.0 39.2 %shard_map.64 = bf16[64,1024]{1,0:T(8,128)(2,1)} custom-call(bf16[8,64,256]{2,1,0:T(8,128)(2,1)} %feat.1, bf16[8,64,256]{2,1,0:T(8,128)(2,1)} %weight.1, f32[1,64]{1,0:T(1,128)} %bitcast.6, f32[1,64]{1,0:T(1,128)} %bitcast.7, s32[60,128]{1,0:T(8,128)} %bitcast.4, s32[60,128]{1,0:T(8,128)} %bitcast.5), custom_call_target="tpu_custom_call" | custom-call | tf_op jit(solution)/shard_map/pallas_call | solution.py:280
  39.2 1.6 %copy.8 = bf16[64,1024]{1,0:T(8,128)(2,1)} copy(bf16[64,1024]{1,0:T(8,128)(2,1)} %shard_map.64) | data formatting | bytes 262144

commit v3 on v2

--- a/solution.py
+++ b/solution.py
@@ -48,7 +48,7 @@
     ny, nz,
     feat, weight, gain, bias, send, recv, out,
     local, packs, weights, gain_row, bias_row, send_tab, recv_tab, back, own, pay, inc, message, pair, held,
-    local_sem, side_send, side_recv, own_send, own_recv, pay_send, pay_recv, stat_send, stat_recv,
+    entered, local_sem, side_send, side_recv, own_send, own_recv, pay_send, pay_recv, stat_send, stat_recv,
 ):
     vox = lax.axis_index("vox")
     ch = lax.axis_index("ch")
@@ -63,7 +63,13 @@
     sibling = vox + 1 - 2 * core
     steps = [(min(a, ny - a) + min(b, nz - b), a, b) for a in range(ny) for b in range(nz)]
     steps = sorted(steps, reverse=True)[:-1]
-    chips = [(lax.rem(y + a, ny) * nz + lax.rem(z + b, nz)) * 2 + core for _, a, b in steps]
+
+    def chip(a, b):
+        return (lax.rem(y + a + ny, ny) * nz + lax.rem(z + b + nz, nz)) * 2 + core
+
+    chips = [chip(a, b) for _, a, b in steps]
+    ring = {d: [chip(d, 0), chip(-d, 0), chip(0, d), chip(0, -d)] for d in (1, 2)}
+    line = [chip(a, 0) for a in range(1, ny)]
 
     def rows_of(source, first=0, size=part):
         return pl.ds(pl.multiple_of(source * part + first, 16), size)
@@ -80,7 +86,7 @@
     barrier = pltpu.get_barrier_semaphore()
     for peer in x_peer[1:]:
         pl.semaphore_signal(barrier, inc=1, device_id={"ch": peer}, device_id_type=MESH)
-    greeted = list(ahead.values()) + [sibling] + chips
+    greeted = list(ahead.values()) + [sibling] + ring[1]
     for peer in greeted:
         pl.semaphore_signal(barrier, inc=1, device_id={"vox": peer}, device_id_type=MESH)
 
@@ -122,19 +128,28 @@
         block = packs.at[i, rows_of(source, first, size)]
         return pltpu.make_async_remote_copy(
             src_ref=block, dst_ref=block, send_sem=own_send.at[way, i - 1], recv_sem=own_recv.at[way, i - 1],
-            device_id={"ch": x_peer[1 if way % 2 == 0 else nx - 1]}, device_id_type=MESH,
+            device_id={"ch": x_peer[(1, nx - 1, 1, nx - 1, 2)[way]]}, device_id_type=MESH,
         )
 
+    ways = [None, (0, 1), (0, 1), (4, 0, 1)]
     half = part // 2
     loads[1].wait()
     pack(0)
     pl.semaphore_wait(barrier, nx - 1 + len(greeted))
+
+    def tell(step, peers):
+        for peer in peers:
+            pl.semaphore_signal(entered.at[step], inc=1, device_id={"vox": peer}, device_id_type=MESH)
+
+    tell(0, ring[1])
     for d in (2, 1, 3):
         side_copy(d, ch).start()
     for i in range(1, PACKS):
         pack(i)
-        own_copy(i, 0, ch).start()
-        own_copy(i, 1, ch).start()
+        for way in ways[i]:
+            own_copy(i, way, ch).start()
+    pl.semaphore_wait(entered.at[0], len(ring[1]))
+    tell(1, ring[2])
 
     place = iota((1, SIDE), 1).astype(F32)
     mirrored = SIDE - 1.0 - place
@@ -181,7 +196,7 @@
         own_copy(i, 1, x_peer[1]).wait_recv()
         own_copy(i, 3, x_peer[1], half, half).start()
 
-    hits = fill(0, GROUP_ROWS, hits)
+    hits = fill(0, blocks, hits)
     loads[3].wait()
     for d in range(1, nx):
         side_copy(d, x_peer[nx - d]).wait_recv()
@@ -199,23 +214,29 @@
             )
             moves[-1].start()
     pass_on(1)
-    hits = fill(GROUP_ROWS, blocks, hits)
+    pl.semaphore_wait(entered.at[1], len(ring[2]))
+    tell(2, line)
     pass_on(2)
-    pass_on(3)
     live = jnp.where(jnp.sum(hits, axis=0, keepdims=True) > 0.0, 1.0, 0.0)
     number = jnp.sum(live, axis=1, keepdims=True)
 
-    for i in range(1, PACKS):
+    def gathered(i):
+        sums = jnp.dot(convolve(i), back[(i - 1) * SIDE : i * SIDE], preferred_element_type=F32)
+        own[...] = sums if i == 1 else own[...] + sums
+
+    for i in (1, 2):
         own_copy(i, 2, x_peer[2], 0, half).wait_recv()
         own_copy(i, 3, x_peer[2], half, half).wait_recv()
-        sums = jnp.dot(convolve(i), back[(i - 1) * SIDE : i * SIDE], preferred_element_type=F32)
-        own[...] = sums if i == 1 else own[...] + sums
+        gathered(i)
+    base = GROUP_ROWS * LANES
     for move, slot in zip(moves, (0, 3, 1, 2)):
         move.wait_recv()
-    base = GROUP_ROWS * LANES
-    for slot in (0, 1, 3, 2):
         matrix = back[base + slot * SIDE : base + (slot + 1) * SIDE]
         own[...] += jnp.dot(inc[slot], matrix, preferred_element_type=F32)
+    own_copy(3, 0, x_peer[nx - 1]).wait_recv()
+    own_copy(3, 1, x_peer[1]).wait_recv()
+    own_copy(3, 4, x_peer[2]).wait_recv()
+    gathered(3)
 
     coarse = own[...]
     total = jnp.sum(coarse * live, axis=1, keepdims=True)
@@ -232,6 +253,7 @@
     swap.start()
     swap.wait_recv()
     message[1] = merge(message[0], pair[...])
+    pl.semaphore_wait(entered.at[2], len(line))
     for j, peer in enumerate(chips):
         pltpu.make_async_remote_copy(
             src_ref=message.at[1], dst_ref=held.at[j], send_sem=stat_send.at[1], recv_sem=stat_recv.at[1],
@@ -255,15 +277,16 @@
     rows = jnp.concatenate([rows, jnp.zeros((8, LANES - width), F32)], axis=1)
     rows = jnp.concatenate([rows, jnp.zeros((LANES - 8, LANES), F32)], axis=0).T
     mean, scale, offset = (rows[:width, i : i + 1] for i in range(3))
-    out[...] = (jnp.maximum((coarse - mean) * scale + offset, 0.0) * live).astype(out.dtype)
+    out[...] = (((coarse - mean) * scale + offset) * live).astype(out.dtype)
 
     for d in range(1, nx):
         side_copy(d, ch).wait_send()
     for i in range(1, PACKS):
-        own_copy(i, 0, ch).wait_send()
-        own_copy(i, 1, ch).wait_send()
-        own_copy(i, 2, x_peer[nx - 1], 0, half).wait_send()
-        own_copy(i, 3, x_peer[1], half, half).wait_send()
+        for way in ways[i]:
+            own_copy(i, way, ch).wait_send()
+        if i < 3:
+            own_copy(i, 2, x_peer[nx - 1], 0, half).wait_send()
+            own_copy(i, 3, x_peer[1], half, half).wait_send()
     for move in moves:
         move.wait_send()
     swap.wait_send()
@@ -277,7 +300,7 @@
         hbm = pl.BlockSpec(memory_space=pltpu.HBM)
         vmem = pl.BlockSpec(memory_space=pltpu.VMEM)
         table = (SPAN * GROUP_ROWS, LANES)
-        return pl.pallas_call(
+        normed = pl.pallas_call(
             functools.partial(kernel, ny, nz),
             out_shape=jax.ShapeDtypeStruct((width, COARSE), BF16),
             in_specs=[hbm] * 6,
@@ -297,11 +320,12 @@
                 pltpu.VMEM((2, 2, LANES), F32),
                 pltpu.VMEM((2, LANES), F32),
                 pltpu.VMEM((ny * nz - 1, 2, LANES), F32),
+                pltpu.SemaphoreType.REGULAR((3,)),
                 pltpu.SemaphoreType.DMA((6,)),
                 pltpu.SemaphoreType.DMA((3,)),
                 pltpu.SemaphoreType.DMA((3,)),
-                pltpu.SemaphoreType.DMA((4, PACKS - 1)),
-                pltpu.SemaphoreType.DMA((4, PACKS - 1)),
+                pltpu.SemaphoreType.DMA((5, PACKS - 1)),
+                pltpu.SemaphoreType.DMA((5, PACKS - 1)),
                 pltpu.SemaphoreType.DMA((4,)),
                 pltpu.SemaphoreType.DMA((4,)),
                 pltpu.SemaphoreType.DMA((2,)),
@@ -318,6 +342,7 @@
             send_row.reshape(table),
             recv_row.reshape(table),
         )
+        return jnp.maximum(normed, 0)
 
     in_specs = (P("vox", "ch", None), P(None, "ch", None), P("ch"), P("ch"), P("vox"), P("vox"))
     out_specs = P("ch", "vox")

time: 40.9 us -> 39 us (0.954)
  Pallas kernels: 39.2 us -> 37.3 us
  other arithmetic: 0 us -> 1.57 us
  local copies, waits for them, and re-layouts: 1.57 us -> 0 us
    pallas_call x1, Pallas kernels: 39.2 us -> 37.3 us  [shards(): pl.pallas_call(functools.partial(kernel, ny, nz), out_shape=jax.ShapeDtyp...]
    max x0 -> x1, other arithmetic: none -> 1.57 us  [shards(): return jnp.maximum(normed, 0)]
    unnamed x1 -> x0, local copies, waits for them, and re-layouts: 1.57 us -> none
where the time goes in v3:
time: 39 us; the launch traced here: 38.8 us
  Pallas kernels  37.3 us (96%)
  other arithmetic  1.57 us (4%)
    pallas_call x1, Pallas kernels, shards(): pl.pallas_call(functools.partial(kernel, ny, nz), out_shape=jax.ShapeDtyp...  37.3 us
    max x1, other arithmetic, shards(): return jnp.maximum(normed, 0)  1.57 us

profile of v3, /device:TPU:1, one launch (start us, length us, event | category | flops | bytes accessed | tf_op | source)
XLA Modules:
  0.0 38.8 jit_solution(8278014723172543597)
XLA Ops:
  0.0 37.3 %shard_map.64 = bf16[64,1024]{1,0:T(8,128)(2,1)} custom-call(bf16[8,64,256]{2,1,0:T(8,128)(2,1)} %feat.1, bf16[8,64,256]{2,1,0:T(8,128)(2,1)} %weight.1, f32[1,64]{1,0:T(1,128)} %bitcast.6, f32[1,64]{1,0:T(1,128)} %bitcast.7, s32[60,128]{1,0:T(8,128)} %bitcast.4, s32[60,128]{1,0:T(8,128)} %bitcast.5), custom_call_target="tpu_custom_call" | custom-call | tf_op jit(solution)/shard_map/pallas_call | solution.py:303
  37.3 1.6 %broadcast_maximum_fusion = bf16[64,1024]{1,0:T(8,128)(2,1)} fusion(bf16[64,1024]{1,0:T(8,128)(2,1)} %shard_map.64), kind=kLoop, calls=%fused_computation | loop fusion | flops 65536 | bytes 262144 | tf_op jit(solution)/shard_map/max | solution.py:345

commit v4 on v3

--- a/solution.py
+++ b/solution.py
@@ -19,6 +19,7 @@
 GROUP_ROWS = CAP // LANES
 PACKS = OFFS * FK // SIDE
 EPSILON = 1e-05
+FAR = 6
 BF16 = jnp.bfloat16
 F32 = jnp.float32
 
@@ -42,6 +43,11 @@
     lane = iota(gap.shape, 1)
     gap = jnp.where(lane < LANES // 2, 0.0, pltpu.roll(gap, LANES // 2, 1))
     return jnp.concatenate([first[0:1] + second[0:1] + gap, number], axis=0)
+
+
+def chip_steps(ny, nz):
+    steps = [(min(a, ny - a) + min(b, nz - b), a, b) for a in range(ny) for b in range(nz)]
+    return sorted(steps, reverse=True)[:-1]
 
 
 def kernel(
@@ -61,13 +67,13 @@
     x_peer = [lax.rem(ch + d, nx) for d in range(nx)]
     ahead = {d: lax.rem(vox + d + nv, nv) for d in (-2, -1, 1, 2)}
     sibling = vox + 1 - 2 * core
-    steps = [(min(a, ny - a) + min(b, nz - b), a, b) for a in range(ny) for b in range(nz)]
-    steps = sorted(steps, reverse=True)[:-1]
+    steps = chip_steps(ny, nz)
 
     def chip(a, b):
         return (lax.rem(y + a + ny, ny) * nz + lax.rem(z + b + nz, nz)) * 2 + core
 
     chips = [chip(a, b) for _, a, b in steps]
+    far = sum(distance >= FAR for distance, _, _ in steps)
     ring = {d: [chip(d, 0), chip(-d, 0), chip(0, d), chip(0, -d)] for d in (1, 2)}
     line = [chip(a, 0) for a in range(1, ny)]
 
@@ -128,10 +134,9 @@
         block = packs.at[i, rows_of(source, first, size)]
         return pltpu.make_async_remote_copy(
             src_ref=block, dst_ref=block, send_sem=own_send.at[way, i - 1], recv_sem=own_recv.at[way, i - 1],
-            device_id={"ch": x_peer[(1, nx - 1, 1, nx - 1, 2)[way]]}, device_id_type=MESH,
+            device_id={"ch": x_peer[1 if way % 2 == 0 else nx - 1]}, device_id_type=MESH,
         )
 
-    ways = [None, (0, 1), (0, 1), (4, 0, 1)]
     half = part // 2
     loads[1].wait()
     pack(0)
@@ -146,8 +151,8 @@
         side_copy(d, ch).start()
     for i in range(1, PACKS):
         pack(i)
-        for way in ways[i]:
-            own_copy(i, way, ch).start()
+        own_copy(i, 0, ch).start()
+        own_copy(i, 1, ch).start()
     pl.semaphore_wait(entered.at[0], len(ring[1]))
     tell(1, ring[2])
 
@@ -217,6 +222,7 @@
     pl.semaphore_wait(entered.at[1], len(ring[2]))
     tell(2, line)
     pass_on(2)
+    pass_on(3)
     live = jnp.where(jnp.sum(hits, axis=0, keepdims=True) > 0.0, 1.0, 0.0)
     number = jnp.sum(live, axis=1, keepdims=True)
 
@@ -233,9 +239,10 @@
         move.wait_recv()
         matrix = back[base + slot * SIDE : base + (slot + 1) * SIDE]
         own[...] += jnp.dot(inc[slot], matrix, preferred_element_type=F32)
-    own_copy(3, 0, x_peer[nx - 1]).wait_recv()
-    own_copy(3, 1, x_peer[1]).wait_recv()
-    own_copy(3, 4, x_peer[2]).wait_recv()
+    pl.semaphore_wait(entered.at[2], len(line))
+    tell(3, [sibling])
+    own_copy(3, 2, x_peer[2], 0, half).wait_recv()
+    own_copy(3, 3, x_peer[2], half, half).wait_recv()
     gathered(3)
 
     coarse = own[...]
@@ -251,17 +258,24 @@
         device_id={"vox": sibling}, device_id_type=MESH,
     )
     swap.start()
+
+    def share(step, slot, peer):
+        pltpu.make_async_remote_copy(
+            src_ref=message.at[step], dst_ref=held.at[slot], send_sem=stat_send.at[1], recv_sem=stat_recv.at[1],
+            device_id={"vox": peer}, device_id_type=MESH,
+        ).start()
+
+    pl.semaphore_wait(entered.at[3], 1)
+    for j in range(far):
+        share(0, 2 * j, chips[j])
+        share(0, 2 * j + 1, chips[j] + 1 - 2 * core)
     swap.wait_recv()
     message[1] = merge(message[0], pair[...])
-    pl.semaphore_wait(entered.at[2], len(line))
-    for j, peer in enumerate(chips):
-        pltpu.make_async_remote_copy(
-            src_ref=message.at[1], dst_ref=held.at[j], send_sem=stat_send.at[1], recv_sem=stat_recv.at[1],
-            device_id={"vox": peer}, device_id_type=MESH,
-        ).start()
+    for j in range(far, len(chips)):
+        share(1, far + j, chips[j])
     pltpu.make_async_copy(held, held, stat_recv.at[1]).wait()
 
-    parts = [message[1]] + [held[j] for j in range(len(chips))]
+    parts = [message[1]] + [held[j] for j in range(far + len(chips))]
     sums = sum(parts)
     number = jnp.maximum(sums[1:2], 1.0)
     mean = sums[0:1] / number
@@ -282,11 +296,10 @@
     for d in range(1, nx):
         side_copy(d, ch).wait_send()
     for i in range(1, PACKS):
-        for way in ways[i]:
-            own_copy(i, way, ch).wait_send()
-        if i < 3:
-            own_copy(i, 2, x_peer[nx - 1], 0, half).wait_send()
-            own_copy(i, 3, x_peer[1], half, half).wait_send()
+        own_copy(i, 0, ch).wait_send()
+        own_copy(i, 1, ch).wait_send()
+        own_copy(i, 2, x_peer[nx - 1], 0, half).wait_send()
+        own_copy(i, 3, x_peer[1], half, half).wait_send()
     for move in moves:
         move.wait_send()
     swap.wait_send()
@@ -294,6 +307,8 @@
 
 
 def solution(mesh, ny=8, nz=8):
+    messages = sum(2 if distance >= FAR else 1 for distance, _, _ in chip_steps(ny, nz))
+
     def shards(fine_feat, conv_weight, norm_gain, norm_bias, send_row, recv_row):
         offsets, width, channels = conv_weight.shape
         part = fine_feat.shape[1]
@@ -302,7 +317,7 @@
         table = (SPAN * GROUP_ROWS, LANES)
         normed = pl.pallas_call(
             functools.partial(kernel, ny, nz),
-            out_shape=jax.ShapeDtypeStruct((width, COARSE), BF16),
+            out_shape=pltpu.VMEM((width, COARSE), BF16),
             in_specs=[hbm] * 6,
             out_specs=vmem,
             scratch_shapes=[
@@ -319,13 +334,13 @@
                 pltpu.VMEM((4, width, SIDE), BF16),
                 pltpu.VMEM((2, 2, LANES), F32),
                 pltpu.VMEM((2, LANES), F32),
-                pltpu.VMEM((ny * nz - 1, 2, LANES), F32),
-                pltpu.SemaphoreType.REGULAR((3,)),
+                pltpu.VMEM((messages, 2, LANES), F32),
+                pltpu.SemaphoreType.REGULAR((4,)),
                 pltpu.SemaphoreType.DMA((6,)),
                 pltpu.SemaphoreType.DMA((3,)),
                 pltpu.SemaphoreType.DMA((3,)),
-                pltpu.SemaphoreType.DMA((5, PACKS - 1)),
-                pltpu.SemaphoreType.DMA((5, PACKS - 1)),
+                pltpu.SemaphoreType.DMA((4, PACKS - 1)),
+                pltpu.SemaphoreType.DMA((4, PACKS - 1)),
                 pltpu.SemaphoreType.DMA((4,)),
                 pltpu.SemaphoreType.DMA((4,)),
                 pltpu.SemaphoreType.DMA((2,)),

time: 39 us -> 36.4 us (0.933)
  Pallas kernels: 37.3 us -> 35.6 us
  other arithmetic: 1.57 us -> 0.67 us
    pallas_call x1, Pallas kernels: 37.3 us -> 35.6 us  [shards(): pl.pallas_call(functools.partial(kernel, ny, nz), out_shape=pltpu.VMEM((w...]
    max x1, other arithmetic: 1.57 us -> 0.67 us  [shards(): return jnp.maximum(normed, 0)]
where the time goes in v4:
time: 36.4 us; the launch traced here: 36.3 us
  Pallas kernels  35.6 us (98%)
  other arithmetic  0.67 us (2%)
    pallas_call x1, Pallas kernels, shards(): pl.pallas_call(functools.partial(kernel, ny, nz), out_shape=pltpu.VMEM((w...  35.6 us

profile of v4, /device:TPU:1, one launch (start us, length us, event | category | flops | bytes accessed | tf_op | source)
XLA Modules:
  0.0 36.3 jit_solution(1694464195861973473)
XLA Ops:
  0.0 35.6 %shard_map.64 = bf16[64,1024]{1,0:T(8,128)(2,1)S(1)} custom-call(bf16[8,64,256]{2,1,0:T(8,128)(2,1)} %feat.1, bf16[8,64,256]{2,1,0:T(8,128)(2,1)} %weight.1, f32[1,64]{1,0:T(1,128)} %bitcast.6, f32[1,64]{1,0:T(1,128)} %bitcast.7, s32[60,128]{1,0:T(8,128)} %bitcast.4, s32[60,128]{1,0:T(8,128)} %bitcast.5), custom_call_target="tpu_custom_call" | custom-call | tf_op jit(solution)/shard_map/pallas_call | solution.py:318
  35.6 0.7 %broadcast_maximum_fusion = bf16[64,1024]{1,0:T(8,128)(2,1)} fusion(bf16[64,1024]{1,0:T(8,128)(2,1)S(1)} %shard_map.64), kind=kLoop, calls=%fused_computation | loop fusion | flops 65536 | bytes 262144 | tf_op jit(solution)/shard_map/max | solution.py:360

commit v5 on v4

--- a/solution.py
+++ b/solution.py
@@ -80,6 +80,13 @@
     def rows_of(source, first=0, size=part):
         return pl.ds(pl.multiple_of(source * part + first, 16), size)
 
+    barrier = pltpu.get_barrier_semaphore()
+    for peer in (x_peer[2], x_peer[1], x_peer[nx - 1]):
+        pl.semaphore_signal(barrier, inc=1, device_id={"ch": peer}, device_id_type=MESH)
+    greeted = list(ahead.values()) + [sibling] + ring[1]
+    for peer in greeted:
+        pl.semaphore_signal(barrier, inc=1, device_id={"vox": peer}, device_id_type=MESH)
+
     loads = [
         pltpu.make_async_copy(src, dst, local_sem.at[i])
         for i, (src, dst) in enumerate(
@@ -88,13 +95,6 @@
     ]
     for load in loads:
         load.start()
-
-    barrier = pltpu.get_barrier_semaphore()
-    for peer in x_peer[1:]:
-        pl.semaphore_signal(barrier, inc=1, device_id={"ch": peer}, device_id_type=MESH)
-    greeted = list(ahead.values()) + [sibling] + ring[1]
-    for peer in greeted:
-        pl.semaphore_signal(barrier, inc=1, device_id={"vox": peer}, device_id_type=MESH)
 
     loads[0].wait()
     side_ids = (0, 1, 3, 4)
@@ -146,9 +146,9 @@
         for peer in peers:
             pl.semaphore_signal(entered.at[step], inc=1, device_id={"vox": peer}, device_id_type=MESH)
 
-    tell(0, ring[1])
     for d in (2, 1, 3):
         side_copy(d, ch).start()
+    tell(0, ring[1])
     for i in range(1, PACKS):
         pack(i)
         own_copy(i, 0, ch).start()
@@ -261,7 +261,7 @@
 
     def share(step, slot, peer):
         pltpu.make_async_remote_copy(
-            src_ref=message.at[step], dst_ref=held.at[slot], send_sem=stat_send.at[1], recv_sem=stat_recv.at[1],
+            src_ref=message.at[step], dst_ref=held.at[pl.ds(2 * slot + 2, 2)], send_sem=stat_send.at[1], recv_sem=stat_recv.at[1],
             device_id={"vox": peer}, device_id_type=MESH,
         ).start()
 
@@ -271,21 +271,23 @@
         share(0, 2 * j + 1, chips[j] + 1 - 2 * core)
     swap.wait_recv()
     message[1] = merge(message[0], pair[...])
+    held[0:2] = message[1]
     for j in range(far, len(chips)):
         share(1, far + j, chips[j])
-    pltpu.make_async_copy(held, held, stat_recv.at[1]).wait()
-
-    parts = [message[1]] + [held[j] for j in range(far + len(chips))]
-    sums = sum(parts)
-    number = jnp.maximum(sums[1:2], 1.0)
-    mean = sums[0:1] / number
-    gaps = jnp.zeros((1, LANES), F32)
-    for p in parts:
-        gap = p[0:1] / jnp.maximum(p[1:2], 1.0) - mean
-        gaps = gaps + gap * gap * p[1:2]
+    arrived = held.at[pl.ds(2, held.shape[0] - 2)]
+    pltpu.make_async_copy(arrived, arrived, stat_recv.at[1]).wait()
+
+    rows = held[...]
+    below = pltpu.roll(rows, rows.shape[0] - 1, 0)
+    first = iota(rows.shape, 0) % 2 == 0
+    sums = jnp.sum(jnp.where(first, rows, 0.0), axis=0, keepdims=True)
+    number = jnp.maximum(jnp.sum(jnp.where(first, below, 0.0), axis=0, keepdims=True), 1.0)
+    mean = sums / number
+    gaps = rows / jnp.maximum(below, 1.0) - mean
+    gaps = jnp.sum(jnp.where(first, gaps * gaps * below, 0.0), axis=0, keepdims=True)
     loads[4].wait()
     loads[5].wait()
-    variance = (pltpu.roll(sums[0:1], LANES // 2, 1) + gaps) / number
+    variance = (pltpu.roll(sums, LANES // 2, 1) + gaps) / number
     scale = lax.rsqrt(variance + EPSILON)[:, :width] * gain_row[...]
     rows = jnp.concatenate([mean[:, :width], scale, bias_row[...], jnp.zeros((5, width), F32)], axis=0)
     rows = jnp.concatenate([rows, jnp.zeros((8, LANES - width), F32)], axis=1)
@@ -303,7 +305,7 @@
     for move in moves:
         move.wait_send()
     swap.wait_send()
-    pltpu.make_async_copy(held, held, stat_send.at[1]).wait()
+    pltpu.make_async_copy(arrived, arrived, stat_send.at[1]).wait()
 
 
 def solution(mesh, ny=8, nz=8):
@@ -334,7 +336,7 @@
                 pltpu.VMEM((4, width, SIDE), BF16),
                 pltpu.VMEM((2, 2, LANES), F32),
                 pltpu.VMEM((2, LANES), F32),
-                pltpu.VMEM((messages, 2, LANES), F32),
+                pltpu.VMEM((2 * messages + 2, LANES), F32),
                 pltpu.SemaphoreType.REGULAR((4,)),
                 pltpu.SemaphoreType.DMA((6,)),
                 pltpu.SemaphoreType.DMA((3,)),

time: 36.4 us -> 36.4 us (level)
  no operation moved by 1% of the time
where the time goes in v5:
time: 36.4 us; the launch traced here: 36.3 us
  Pallas kernels  35.6 us (98%)
  other arithmetic  0.67 us (2%)
    pallas_call x1, Pallas kernels, shards(): pl.pallas_call(functools.partial(kernel, ny, nz), out_shape=pltpu.VMEM((w...  35.6 us

profile of v5, /device:TPU:1, one launch (start us, length us, event | category | flops | bytes accessed | tf_op | source)
XLA Modules:
  0.0 36.3 jit_solution(13355819836226238897)
XLA Ops:
  0.0 35.6 %shard_map.64 = bf16[64,1024]{1,0:T(8,128)(2,1)S(1)} custom-call(bf16[8,64,256]{2,1,0:T(8,128)(2,1)} %feat.1, bf16[8,64,256]{2,1,0:T(8,128)(2,1)} %weight.1, f32[1,64]{1,0:T(1,128)} %bitcast.6, f32[1,64]{1,0:T(1,128)} %bitcast.7, s32[60,128]{1,0:T(8,128)} %bitcast.4, s32[60,128]{1,0:T(8,128)} %bitcast.5), custom_call_target="tpu_custom_call" | custom-call | tf_op jit(solution)/shard_map/pallas_call | solution.py:320
  35.6 0.7 %broadcast_maximum_fusion = bf16[64,1024]{1,0:T(8,128)(2,1)} fusion(bf16[64,1024]{1,0:T(8,128)(2,1)S(1)} %shard_map.64), kind=kLoop, calls=%fused_computation | loop fusion | flops 65536 | bytes 262144 | tf_op jit(solution)/shard_map/max | solution.py:362

commit v6 on v5

--- a/solution.py
+++ b/solution.py
@@ -243,9 +243,8 @@
     tell(3, [sibling])
     own_copy(3, 2, x_peer[2], 0, half).wait_recv()
     own_copy(3, 3, x_peer[2], half, half).wait_recv()
-    gathered(3)
-
-    coarse = own[...]
+
+    coarse = own[...] + jnp.dot(convolve(3), back[2 * SIDE : 3 * SIDE], preferred_element_type=F32)
     total = jnp.sum(coarse * live, axis=1, keepdims=True)
     centred = (coarse - total / jnp.maximum(number, 1.0)) * live
     spread = jnp.sum(centred * centred, axis=1, keepdims=True)

time: 36.4 us -> 36.4 us (level)
  no operation moved by 1% of the time
where the time goes in v6:
time: 36.4 us; the launch traced here: 36.3 us
  Pallas kernels  35.6 us (98%)
  other arithmetic  0.67 us (2%)
    pallas_call x1, Pallas kernels, shards(): pl.pallas_call(functools.partial(kernel, ny, nz), out_shape=pltpu.VMEM((w...  35.6 us

profile of v6, /device:TPU:1, one launch (start us, length us, event | category | flops | bytes accessed | tf_op | source)
XLA Modules:
  0.0 36.3 jit_solution(13355819836226238897)
XLA Ops:
  0.0 35.6 %shard_map.64 = bf16[64,1024]{1,0:T(8,128)(2,1)S(1)} custom-call(bf16[8,64,256]{2,1,0:T(8,128)(2,1)} %feat.1, bf16[8,64,256]{2,1,0:T(8,128)(2,1)} %weight.1, f32[1,64]{1,0:T(1,128)} %bitcast.6, f32[1,64]{1,0:T(1,128)} %bitcast.7, s32[60,128]{1,0:T(8,128)} %bitcast.4, s32[60,128]{1,0:T(8,128)} %bitcast.5), custom_call_target="tpu_custom_call" | custom-call | tf_op jit(solution)/shard_map/pallas_call | solution.py:319
  35.6 0.7 %broadcast_maximum_fusion = bf16[64,1024]{1,0:T(8,128)(2,1)} fusion(bf16[64,1024]{1,0:T(8,128)(2,1)S(1)} %shard_map.64), kind=kLoop, calls=%fused_computation | loop fusion | flops 65536 | bytes 262144 | tf_op jit(solution)/shard_map/max | solution.py:361
